TPU v7x, 32 devices: a whole 2x2x4 slice. The times are simulated.
32 devices in a mesh: phase: 4 (over z), rows: 8 (over y, x, core).
Axes of the slice: x: 2, y: 2, z: 4, core: 2. Of those that a mesh axis runs over, the one named last changes fastest.
Arguments:
- start: bfloat16 [4, 8192, 256], P('phase', 'rows')
- blocks: bfloat16 [4, 64, 4, 128, 128], P('phase', 'rows')
- cols: int32 [4, 64, 4], P('phase', 'rows'), may hold values from 0 to 63, as said below
- counts: int32 [4, 64], P('phase', 'rows'), may hold values from 1 to 4, as said below
Outputs:
- basis: float32 [4, 8192, 256], P('phase', 'rows')
- factor: float32 [4, 256, 256], P('phase')
Inputs may be any that keep to these rules, and one draw needn't show every extreme that they name: cols[q, i, 0] = i; the other slots of block row i name distinct block rows (i + o) mod 64 with 1 <= |o| <= 2. Block row i of section q uses its first counts[q, i] slots; every section has a block row that uses all 4.
All inputs are finite; a program needn't handle non-finite values.
Results may differ from a plain program's by a relative error of at most 0.012.
Values may be sent and summed in bfloat16 or wider, within the bound.
A program may use at most 64 MiB of HBM per device.

v0:
```python
import jax
import jax.numpy as jnp
from jax import lax
from jax.sharding import PartitionSpec as P

HB = 2


def with_halo(array, sides, width):
    for axis, dim in sides:
        peers, length = (lax.axis_size(axis), array.shape[dim])
        up = [(i, (i + 1) % peers) for i in range(peers)]
        down = [(j, i) for i, j in up]
        last = lax.slice_in_dim(array, length - width, length, axis=dim)
        leading = lax.slice_in_dim(array, 0, width, axis=dim)
        before = lax.ppermute(last, axis, up)
        after = lax.ppermute(leading, axis, down)
        array = jnp.concatenate([before, array, after], axis=dim)
    return array


def passed_along(value, axis, steps):
    count = lax.axis_size(axis)
    pairs = [(source, (source + steps) % count) for source in range(count)]
    return lax.ppermute(value, axis, pairs)


def body(start, blocks, cols, counts):
    block_rows = blocks.shape[1]
    slot_count = blocks.shape[2]
    tile_size = blocks.shape[3]
    rows_here = start.shape[1]
    owners = lax.axis_size("rows")
    sections = lax.axis_size("phase")
    total_blocks = block_rows * owners
    first_block = lax.axis_index("rows") * block_rows
    local_index = jnp.mod(cols[0] - first_block + HB, total_blocks)
    live_slots = jnp.arange(slot_count, dtype=jnp.int32)[None, :] < counts[0][:, None]
    zero_value = jnp.zeros((), jnp.bfloat16)
    kept_blocks = jnp.where(live_slots[:, :, None, None], blocks[0], zero_value)
    rim_rows = HB * tile_size

    def advance(current):
        columns = current.shape[1]
        extended = with_halo(current, (("rows", 0),), rim_rows)
        row_tiles = extended.reshape(block_rows + 2 * HB, tile_size, columns)
        picked = row_tiles[local_index]
        product = jnp.einsum(
            "ijab,ijbk->iak", kept_blocks, picked, preferred_element_type=jnp.float32
        )
        return product.reshape(rows_here, columns).astype(jnp.bfloat16)

    half_width = start.shape[2] // 2

    def turn_two(turn_index, both_panels):
        left_panel = passed_along(advance(both_panels[0]), "phase", 1)
        right_panel = passed_along(advance(both_panels[1]), "phase", 1)
        return (left_panel, right_panel)

    left_panel, right_panel = lax.fori_loop(
        0, sections, turn_two, (start[0][:, :half_width], start[0][:, half_width:])
    )
    arrived = jnp.concatenate([left_panel, right_panel], axis=1)
    gram_term = lax.dot_general(
        arrived, arrived, (((0,), (0,)), ((), ())), preferred_element_type=jnp.float32
    )
    gram_total = lax.psum(gram_term.astype(jnp.bfloat16), "rows").astype(jnp.float32) / (
        rows_here * owners
    )
    lower_factor = jnp.linalg.cholesky(gram_total)
    basis_out = jax.scipy.linalg.solve_triangular(
        lower_factor, arrived.astype(jnp.float32).T, lower=True
    ).T
    return (basis_out[None], lower_factor.T[None])


def solution(mesh):
    placed = (
        P("phase", "rows", None),
        P("phase", "rows", None, None, None),
        P("phase", "rows", None),
        P("phase", "rows"),
    )
    return jax.shard_map(
        body,
        mesh=mesh,
        in_specs=placed,
        out_specs=(P("phase", "rows", None), P("phase", None, None)),
        check_vma=False,
    )
```

profile of v0, /device:TPU:0, one launch (start us, length us, event | category | flops | bytes accessed | tf_op | source)
XLA Modules:
  0.0 221.7 jit_solution(468534387700457744)
XLA Ops:
  9.8 86.5 %while.13 = (s32[]{:T(128)}, bf16[1024,128]{1,0:T(8,128)(2,1)S(1)}, bf16[1024,128]{1,0:T(8,128)(2,1)S(1)}, s32[8,4]{0,1:T(4,128)S(1)}, bf16[8,4,128,128]{3,2,1,0:T(8,128)(2,1)S(1)}, /*index=5*/s32[]{:T(128)}) while((s32[]{:T(128)}, bf16[1024,128]{1,0:T(8,128)(2,1)S(1)}, bf16[1024,128]{1,0:T(8,128)(2,1)S(1)}, s32[8,4]{0,1:T(4,128)S(1)}, ...), condition=%wide.region_1.2_spmd, body=%wide.region_0.1_spmd.sunk | while | flops 271058016 | bytes 14161333 | solution.py:60
  9.8 3.4 %collective-permute-start.3 = (bf16[256,128]{1,0:T(8,128)(2,1)S(1)}, bf16[256,128]{1,0:T(8,128)(2,1)S(1)}, u32[]{:S(2)}, u32[]{:S(2)}) collective-permute-start(bf16[256,128]{1,0:T(8,128)(2,1)S(1)} %get-tuple-element.140), channel_id=1, source_target_pairs={{1,0},{2,1},{3,2},{4,3},{5,4},{6,5},{7,6},{0,7},{9,8},{10,9},{11,1... | collective-permute-start | bytes 196616 | tf_op jit(solution)/shard_map/while/body/eval_jaxpr/ppermute | solution.py:17
  13.2 2.7 %collective-permute-start = (bf16[256,128]{1,0:T(8,128)(2,1)S(1)}, bf16[256,128]{1,0:T(8,128)(2,1)S(1)}, u32[]{:S(2)}, u32[]{:S(2)}) collective-permute-start(bf16[256,128]{1,0:T(8,128)(2,1)S(1)} %get-tuple-element.138), channel_id=1, source_target_pairs={{1,0},{2,1},{3,2},{4,3},{5,4},{6,5},{7,6},{0,7},{9,8},{10,9},{11,1... | collective-permute-start | bytes 196616 | tf_op jit(solution)/shard_map/while/body/eval_jaxpr/ppermute | solution.py:17
  16.1 2.3 %collective-permute-done.4 = bf16[256,128]{1,0:T(8,128)(2,1)S(1)} collective-permute-done((bf16[256,128]{1,0:T(8,128)(2,1)S(1)}, bf16[256,128]{1,0:T(8,128)(2,1)S(1)}, u32[]{:S(2)}, u32[]{:S(2)}) %collective-permute-start.4) | collective-permute-done | bytes 65568 | tf_op jit(solution)/shard_map/while/body/eval_jaxpr/ppermute | solution.py:16
  19.6 1.6 collective-permute-start.5
  22.5 1.6 collective-permute-start.2
  24.1 5.1 %collective-permute-done.5 = bf16[1024,128]{1,0:T(8,128)(2,1)S(1)} collective-permute-done((bf16[1024,128]{1,0:T(8,128)(2,1)S(1)}, bf16[1024,128]{1,0:T(8,128)(2,1)S(1)}, u32[]{:S(2)}, u32[]{:S(2)}) %collective-permute-start.5) | collective-permute-done | bytes 262176 | tf_op jit(solution)/shard_map/while/body/eval_jaxpr/ppermute | solution.py:25
  29.1 2.8 %collective-permute-done.2 = bf16[1024,128]{1,0:T(8,128)(2,1)S(1)} collective-permute-done((bf16[1024,128]{1,0:T(8,128)(2,1)S(1)}, bf16[1024,128]{1,0:T(8,128)(2,1)S(1)}, u32[]{:S(2)}, u32[]{:S(2)}) %collective-permute-start.2) | collective-permute-done | bytes 262176 | tf_op jit(solution)/shard_map/while/body/eval_jaxpr/ppermute | solution.py:25
  32.0 3.6 %collective-permute-start.3 = (bf16[256,128]{1,0:T(8,128)(2,1)S(1)}, bf16[256,128]{1,0:T(8,128)(2,1)S(1)}, u32[]{:S(2)}, u32[]{:S(2)}) collective-permute-start(bf16[256,128]{1,0:T(8,128)(2,1)S(1)} %get-tuple-element.140), channel_id=1, source_target_pairs={{1,0},{2,1},{3,2},{4,3},{5,4},{6,5},{7,6},{0,7},{9,8},{10,9},{11,1... | collective-permute-start | bytes 196616 | tf_op jit(solution)/shard_map/while/body/eval_jaxpr/ppermute | solution.py:17
  35.6 2.7 %collective-permute-start = (bf16[256,128]{1,0:T(8,128)(2,1)S(1)}, bf16[256,128]{1,0:T(8,128)(2,1)S(1)}, u32[]{:S(2)}, u32[]{:S(2)}) collective-permute-start(bf16[256,128]{1,0:T(8,128)(2,1)S(1)} %get-tuple-element.138), channel_id=1, source_target_pairs={{1,0},{2,1},{3,2},{4,3},{5,4},{6,5},{7,6},{0,7},{9,8},{10,9},{11,1... | collective-permute-start | bytes 196616 | tf_op jit(solution)/shard_map/while/body/eval_jaxpr/ppermute | solution.py:17
  38.5 2.2 collective-permute-done.4
  44.7 6.3 %collective-permute-done.5 = bf16[1024,128]{1,0:T(8,128)(2,1)S(1)} collective-permute-done((bf16[1024,128]{1,0:T(8,128)(2,1)S(1)}, bf16[1024,128]{1,0:T(8,128)(2,1)S(1)}, u32[]{:S(2)}, u32[]{:S(2)}) %collective-permute-start.5) | collective-permute-done | bytes 262176 | tf_op jit(solution)/shard_map/while/body/eval_jaxpr/ppermute | solution.py:25
  51.0 2.8 %collective-permute-done.2 = bf16[1024,128]{1,0:T(8,128)(2,1)S(1)} collective-permute-done((bf16[1024,128]{1,0:T(8,128)(2,1)S(1)}, bf16[1024,128]{1,0:T(8,128)(2,1)S(1)}, u32[]{:S(2)}, u32[]{:S(2)}) %collective-permute-start.2) | collective-permute-done | bytes 262176 | tf_op jit(solution)/shard_map/while/body/eval_jaxpr/ppermute | solution.py:25
  53.8 3.4 %collective-permute-start.3 = (bf16[256,128]{1,0:T(8,128)(2,1)S(1)}, bf16[256,128]{1,0:T(8,128)(2,1)S(1)}, u32[]{:S(2)}, u32[]{:S(2)}) collective-permute-start(bf16[256,128]{1,0:T(8,128)(2,1)S(1)} %get-tuple-element.140), channel_id=1, source_target_pairs={{1,0},{2,1},{3,2},{4,3},{5,4},{6,5},{7,6},{0,7},{9,8},{10,9},{11,1... | collective-permute-start | bytes 196616 | tf_op jit(solution)/shard_map/while/body/eval_jaxpr/ppermute | solution.py:17
  57.2 2.7 %collective-permute-start = (bf16[256,128]{1,0:T(8,128)(2,1)S(1)}, bf16[256,128]{1,0:T(8,128)(2,1)S(1)}, u32[]{:S(2)}, u32[]{:S(2)}) collective-permute-start(bf16[256,128]{1,0:T(8,128)(2,1)S(1)} %get-tuple-element.138), channel_id=1, source_target_pairs={{1,0},{2,1},{3,2},{4,3},{5,4},{6,5},{7,6},{0,7},{9,8},{10,9},{11,1... | collective-permute-start | bytes 196616 | tf_op jit(solution)/shard_map/while/body/eval_jaxpr/ppermute | solution.py:17
  60.0 1.7 collective-permute-done.4
  63.0 1.4 collective-permute-done.1
  65.7 6.8 %collective-permute-done.5 = bf16[1024,128]{1,0:T(8,128)(2,1)S(1)} collective-permute-done((bf16[1024,128]{1,0:T(8,128)(2,1)S(1)}, bf16[1024,128]{1,0:T(8,128)(2,1)S(1)}, u32[]{:S(2)}, u32[]{:S(2)}) %collective-permute-start.5) | collective-permute-done | bytes 262176 | tf_op jit(solution)/shard_map/while/body/eval_jaxpr/ppermute | solution.py:25
  72.5 2.8 %collective-permute-done.2 = bf16[1024,128]{1,0:T(8,128)(2,1)S(1)} collective-permute-done((bf16[1024,128]{1,0:T(8,128)(2,1)S(1)}, bf16[1024,128]{1,0:T(8,128)(2,1)S(1)}, u32[]{:S(2)}, u32[]{:S(2)}) %collective-permute-start.2) | collective-permute-done | bytes 262176 | tf_op jit(solution)/shard_map/while/body/eval_jaxpr/ppermute | solution.py:25
  75.3 2.8 %collective-permute-start.3 = (bf16[256,128]{1,0:T(8,128)(2,1)S(1)}, bf16[256,128]{1,0:T(8,128)(2,1)S(1)}, u32[]{:S(2)}, u32[]{:S(2)}) collective-permute-start(bf16[256,128]{1,0:T(8,128)(2,1)S(1)} %get-tuple-element.140), channel_id=1, source_target_pairs={{1,0},{2,1},{3,2},{4,3},{5,4},{6,5},{7,6},{0,7},{9,8},{10,9},{11,1... | collective-permute-start | bytes 196616 | tf_op jit(solution)/shard_map/while/body/eval_jaxpr/ppermute | solution.py:17
  78.1 2.7 %collective-permute-start = (bf16[256,128]{1,0:T(8,128)(2,1)S(1)}, bf16[256,128]{1,0:T(8,128)(2,1)S(1)}, u32[]{:S(2)}, u32[]{:S(2)}) collective-permute-start(bf16[256,128]{1,0:T(8,128)(2,1)S(1)} %get-tuple-element.138), channel_id=1, source_target_pairs={{1,0},{2,1},{3,2},{4,3},{5,4},{6,5},{7,6},{0,7},{9,8},{10,9},{11,1... | collective-permute-start | bytes 196616 | tf_op jit(solution)/shard_map/while/body/eval_jaxpr/ppermute | solution.py:17
  81.0 1.7 collective-permute-done.4
  84.0 1.4 collective-permute-done.1
  86.7 6.8 %collective-permute-done.5 = bf16[1024,128]{1,0:T(8,128)(2,1)S(1)} collective-permute-done((bf16[1024,128]{1,0:T(8,128)(2,1)S(1)}, bf16[1024,128]{1,0:T(8,128)(2,1)S(1)}, u32[]{:S(2)}, u32[]{:S(2)}) %collective-permute-start.5) | collective-permute-done | bytes 262176 | tf_op jit(solution)/shard_map/while/body/eval_jaxpr/ppermute | solution.py:25
  93.5 2.8 %collective-permute-done.2 = bf16[1024,128]{1,0:T(8,128)(2,1)S(1)} collective-permute-done((bf16[1024,128]{1,0:T(8,128)(2,1)S(1)}, bf16[1024,128]{1,0:T(8,128)(2,1)S(1)}, u32[]{:S(2)}, u32[]{:S(2)}) %collective-permute-start.2) | collective-permute-done | bytes 262176 | tf_op jit(solution)/shard_map/while/body/eval_jaxpr/ppermute | solution.py:25
  97.5 51.4 %all-reduce.3.cloned.1.call-done = bf16[256,256]{0,1:T(8,128)(2,1)} async-done(((bf16[256,256]{0,1:T(8,128)(2,1)}), bf16[256,256]{0,1:T(8,128)(2,1)}) %all-reduce.3.cloned.1.call-update) | async-done | bytes 131088 | tf_op jit(solution)/shard_map/psum | solution.py:67
  150.7 11.7 %cholesky.50 = f32[128,128]{1,0:T(8,128)S(1)} custom-call(f32[128,128]{1,0:T(8,128)S(1)} %cholesky.118), custom_call_target="Cholesky" | custom-call | tf_op jit(solution)/shard_map/jit(cholesky)/cholesky | solution.py:70
  162.5 9.8 %custom-call.15 = f32[1,128,128]{1,2,0:T(8,128)S(1)} custom-call(f32[1,128,128]{2,1,0:T(8,128)S(1)} %get-tuple-element.75), custom_call_target="InvertDiagBlocksLowerTriangular" | custom-call | tf_op jit(solution)/shard_map/jit(cholesky)/cholesky | solution.py:70
  172.8 11.7 %cholesky.105 = f32[128,128]{1,0:T(8,128)S(1)} custom-call(f32[128,128]{1,0:T(8,128)S(1)} %convolution_subtract_fusion.1), custom_call_target="Cholesky" | custom-call | tf_op jit(solution)/shard_map/jit(cholesky)/cholesky | solution.py:70
  186.6 3.9 %while.14 = (s32[]{:T(128)}, f32[256,256]{1,0:T(8,128)S(1)}, s32[2,2]{1,0:T(2,128)S(1)}, f32[2,128,128]{2,1,0:T(8,128)S(1)}, s32[]{:T(128)}) while((s32[]{:T(128)}, f32[256,256]{1,0:T(8,128)S(1)}, s32[2,2]{1,0:T(2,128)S(1)}, f32[2,128,128]{2,1,0:T(8,128)S(1)}, s32[]{:T(128)}) %tuple.53), condition=%wide.while_cond, body=%wide.while_body.sunk | while | flops 2 | bytes 131181 | solution.py:71
  187.2 1.4 bitcast_dynamic-update-slice_fusion.2
  190.6 19.9 %custom-call.16 = f32[2,128,128]{1,2,0:T(8,128)S(1)} custom-call(f32[2,128,128]{2,1,0:T(8,128)S(1)} %get-tuple-element.39), custom_call_target="InvertDiagBlocksLowerTriangular" | custom-call | tf_op jit(solution)/shard_map/jit(_solve_triangular)/triangular_solve | solution.py:71
  (114 shorter events, 26.0 us)
Async XLA Ops:
  7.2 1.9 copy-start
  7.2 141.7 %all-reduce.3.cloned.1.call-start = ((), (), s32[]{:S(2)}) async-start(), calls=%async_computation | async-start | bytes 262144 | tf_op jit(solution)/shard_map/psum | solution.py:67
  8.4 0.7 copy-start.3
  9.1 0.7 copy-start.2
  9.8 6.3 %collective-permute-start.3 = (bf16[256,128]{1,0:T(8,128)(2,1)S(1)}, bf16[256,128]{1,0:T(8,128)(2,1)S(1)}, u32[]{:S(2)}, u32[]{:S(2)}) collective-permute-start(bf16[256,128]{1,0:T(8,128)(2,1)S(1)} %get-tuple-element.140), channel_id=1, source_target_pairs={{1,0},{2,1},{3,2},{4,3},{5,4},{6,5},{7,6},{0,7},{9,8},{10,9},{11,1... | collective-permute-start | bytes 196616 | tf_op jit(solution)/shard_map/while/body/eval_jaxpr/ppermute | solution.py:17
  13.2 5.2 %collective-permute-start.4 = (bf16[256,128]{1,0:T(8,128)(2,1)S(1)}, bf16[256,128]{1,0:T(8,128)(2,1)S(1)}, u32[]{:S(2)}, u32[]{:S(2)}) collective-permute-start(bf16[256,128]{1,0:T(8,128)(2,1)S(1)} %get-tuple-element.141), channel_id=1, source_target_pairs={{0,1},{1,2},{2,3},{3,4},{4,5},{5,6},{6,7},{7,0},{8,9},{9,10},{10,1... | collective-permute-start | bytes 196616 | tf_op jit(solution)/shard_map/while/body/eval_jaxpr/ppermute | solution.py:16
  13.2 8.0 %collective-permute-start = (bf16[256,128]{1,0:T(8,128)(2,1)S(1)}, bf16[256,128]{1,0:T(8,128)(2,1)S(1)}, u32[]{:S(2)}, u32[]{:S(2)}) collective-permute-start(bf16[256,128]{1,0:T(8,128)(2,1)S(1)} %get-tuple-element.138), channel_id=1, source_target_pairs={{1,0},{2,1},{3,2},{4,3},{5,4},{6,5},{7,6},{0,7},{9,8},{10,9},{11,1... | collective-permute-start | bytes 196616 | tf_op jit(solution)/shard_map/while/body/eval_jaxpr/ppermute | solution.py:17
  15.9 5.3 %collective-permute-start.1 = (bf16[256,128]{1,0:T(8,128)(2,1)S(1)}, bf16[256,128]{1,0:T(8,128)(2,1)S(1)}, u32[]{:S(2)}, u32[]{:S(2)}) collective-permute-start(bf16[256,128]{1,0:T(8,128)(2,1)S(1)} %get-tuple-element.139), channel_id=1, source_target_pairs={{0,1},{1,2},{2,3},{3,4},{4,5},{5,6},{6,7},{7,0},{8,9},{9,10},{10,1... | collective-permute-start | bytes 196616 | tf_op jit(solution)/shard_map/while/body/eval_jaxpr/ppermute | solution.py:16
  19.6 9.5 %collective-permute-start.5 = (bf16[1024,128]{1,0:T(8,128)(2,1)S(1)}, bf16[1024,128]{1,0:T(8,128)(2,1)S(1)}, u32[]{:S(2)}, u32[]{:S(2)}) collective-permute-start(bf16[1024,128]{1,0:T(8,128)(2,1)S(1)} %bitcast.108), channel_id=1, source_target_pairs={{0,8},{8,16},{16,24},{24,0},{1,9},{9,17},{17,25},{25,1},{2,10},{10... | collective-permute-start | bytes 786440 | tf_op jit(solution)/shard_map/while/body/eval_jaxpr/ppermute | solution.py:25
  22.5 9.5 %collective-permute-start.2 = (bf16[1024,128]{1,0:T(8,128)(2,1)S(1)}, bf16[1024,128]{1,0:T(8,128)(2,1)S(1)}, u32[]{:S(2)}, u32[]{:S(2)}) collective-permute-start(bf16[1024,128]{1,0:T(8,128)(2,1)S(1)} %bitcast.109), channel_id=1, source_target_pairs={{0,8},{8,16},{16,24},{24,0},{1,9},{9,17},{17,25},{25,1},{2,10},{10... | collective-permute-start | bytes 786440 | tf_op jit(solution)/shard_map/while/body/eval_jaxpr/ppermute | solution.py:25
  32.0 6.5 %collective-permute-start.3 = (bf16[256,128]{1,0:T(8,128)(2,1)S(1)}, bf16[256,128]{1,0:T(8,128)(2,1)S(1)}, u32[]{:S(2)}, u32[]{:S(2)}) collective-permute-start(bf16[256,128]{1,0:T(8,128)(2,1)S(1)} %get-tuple-element.140), channel_id=1, source_target_pairs={{1,0},{2,1},{3,2},{4,3},{5,4},{6,5},{7,6},{0,7},{9,8},{10,9},{11,1... | collective-permute-start | bytes 196616 | tf_op jit(solution)/shard_map/while/body/eval_jaxpr/ppermute | solution.py:17
  35.6 5.1 %collective-permute-start.4 = (bf16[256,128]{1,0:T(8,128)(2,1)S(1)}, bf16[256,128]{1,0:T(8,128)(2,1)S(1)}, u32[]{:S(2)}, u32[]{:S(2)}) collective-permute-start(bf16[256,128]{1,0:T(8,128)(2,1)S(1)} %get-tuple-element.141), channel_id=1, source_target_pairs={{0,1},{1,2},{2,3},{3,4},{4,5},{5,6},{6,7},{7,0},{8,9},{9,10},{10,1... | collective-permute-start | bytes 196616 | tf_op jit(solution)/shard_map/while/body/eval_jaxpr/ppermute | solution.py:16
  35.6 6.4 %collective-permute-start = (bf16[256,128]{1,0:T(8,128)(2,1)S(1)}, bf16[256,128]{1,0:T(8,128)(2,1)S(1)}, u32[]{:S(2)}, u32[]{:S(2)}) collective-permute-start(bf16[256,128]{1,0:T(8,128)(2,1)S(1)} %get-tuple-element.138), channel_id=1, source_target_pairs={{1,0},{2,1},{3,2},{4,3},{5,4},{6,5},{7,6},{0,7},{9,8},{10,9},{11,1... | collective-permute-start | bytes 196616 | tf_op jit(solution)/shard_map/while/body/eval_jaxpr/ppermute | solution.py:17
  38.3 4.6 %collective-permute-start.1 = (bf16[256,128]{1,0:T(8,128)(2,1)S(1)}, bf16[256,128]{1,0:T(8,128)(2,1)S(1)}, u32[]{:S(2)}, u32[]{:S(2)}) collective-permute-start(bf16[256,128]{1,0:T(8,128)(2,1)S(1)} %get-tuple-element.139), channel_id=1, source_target_pairs={{0,1},{1,2},{2,3},{3,4},{4,5},{5,6},{6,7},{7,0},{8,9},{9,10},{10,1... | collective-permute-start | bytes 196616 | tf_op jit(solution)/shard_map/while/body/eval_jaxpr/ppermute | solution.py:16
  41.9 9.0 %collective-permute-start.5 = (bf16[1024,128]{1,0:T(8,128)(2,1)S(1)}, bf16[1024,128]{1,0:T(8,128)(2,1)S(1)}, u32[]{:S(2)}, u32[]{:S(2)}) collective-permute-start(bf16[1024,128]{1,0:T(8,128)(2,1)S(1)} %bitcast.108), channel_id=1, source_target_pairs={{0,8},{8,16},{16,24},{24,0},{1,9},{9,17},{17,25},{25,1},{2,10},{10... | collective-permute-start | bytes 786440 | tf_op jit(solution)/shard_map/while/body/eval_jaxpr/ppermute | solution.py:25
  44.1 9.6 %collective-permute-start.2 = (bf16[1024,128]{1,0:T(8,128)(2,1)S(1)}, bf16[1024,128]{1,0:T(8,128)(2,1)S(1)}, u32[]{:S(2)}, u32[]{:S(2)}) collective-permute-start(bf16[1024,128]{1,0:T(8,128)(2,1)S(1)} %bitcast.109), channel_id=1, source_target_pairs={{0,8},{8,16},{16,24},{24,0},{1,9},{9,17},{17,25},{25,1},{2,10},{10... | collective-permute-start | bytes 786440 | tf_op jit(solution)/shard_map/while/body/eval_jaxpr/ppermute | solution.py:25
  53.8 6.2 %collective-permute-start.3 = (bf16[256,128]{1,0:T(8,128)(2,1)S(1)}, bf16[256,128]{1,0:T(8,128)(2,1)S(1)}, u32[]{:S(2)}, u32[]{:S(2)}) collective-permute-start(bf16[256,128]{1,0:T(8,128)(2,1)S(1)} %get-tuple-element.140), channel_id=1, source_target_pairs={{1,0},{2,1},{3,2},{4,3},{5,4},{6,5},{7,6},{0,7},{9,8},{10,9},{11,1... | collective-permute-start | bytes 196616 | tf_op jit(solution)/shard_map/while/body/eval_jaxpr/ppermute | solution.py:17
  57.1 4.6 %collective-permute-start.4 = (bf16[256,128]{1,0:T(8,128)(2,1)S(1)}, bf16[256,128]{1,0:T(8,128)(2,1)S(1)}, u32[]{:S(2)}, u32[]{:S(2)}) collective-permute-start(bf16[256,128]{1,0:T(8,128)(2,1)S(1)} %get-tuple-element.141), channel_id=1, source_target_pairs={{0,1},{1,2},{2,3},{3,4},{4,5},{5,6},{6,7},{7,0},{8,9},{9,10},{10,1... | collective-permute-start | bytes 196616 | tf_op jit(solution)/shard_map/while/body/eval_jaxpr/ppermute | solution.py:16
  57.2 5.9 %collective-permute-start = (bf16[256,128]{1,0:T(8,128)(2,1)S(1)}, bf16[256,128]{1,0:T(8,128)(2,1)S(1)}, u32[]{:S(2)}, u32[]{:S(2)}) collective-permute-start(bf16[256,128]{1,0:T(8,128)(2,1)S(1)} %get-tuple-element.138), channel_id=1, source_target_pairs={{1,0},{2,1},{3,2},{4,3},{5,4},{6,5},{7,6},{0,7},{9,8},{10,9},{11,1... | collective-permute-start | bytes 196616 | tf_op jit(solution)/shard_map/while/body/eval_jaxpr/ppermute | solution.py:17
  59.8 4.6 %collective-permute-start.1 = (bf16[256,128]{1,0:T(8,128)(2,1)S(1)}, bf16[256,128]{1,0:T(8,128)(2,1)S(1)}, u32[]{:S(2)}, u32[]{:S(2)}) collective-permute-start(bf16[256,128]{1,0:T(8,128)(2,1)S(1)} %get-tuple-element.139), channel_id=1, source_target_pairs={{0,1},{1,2},{2,3},{3,4},{4,5},{5,6},{6,7},{7,0},{8,9},{9,10},{10,1... | collective-permute-start | bytes 196616 | tf_op jit(solution)/shard_map/while/body/eval_jaxpr/ppermute | solution.py:16
  62.9 9.5 %collective-permute-start.5 = (bf16[1024,128]{1,0:T(8,128)(2,1)S(1)}, bf16[1024,128]{1,0:T(8,128)(2,1)S(1)}, u32[]{:S(2)}, u32[]{:S(2)}) collective-permute-start(bf16[1024,128]{1,0:T(8,128)(2,1)S(1)} %bitcast.108), channel_id=1, source_target_pairs={{0,8},{8,16},{16,24},{24,0},{1,9},{9,17},{17,25},{25,1},{2,10},{10... | collective-permute-start | bytes 786440 | tf_op jit(solution)/shard_map/while/body/eval_jaxpr/ppermute | solution.py:25
  65.7 9.6 %collective-permute-start.2 = (bf16[1024,128]{1,0:T(8,128)(2,1)S(1)}, bf16[1024,128]{1,0:T(8,128)(2,1)S(1)}, u32[]{:S(2)}, u32[]{:S(2)}) collective-permute-start(bf16[1024,128]{1,0:T(8,128)(2,1)S(1)} %bitcast.109), channel_id=1, source_target_pairs={{0,8},{8,16},{16,24},{24,0},{1,9},{9,17},{17,25},{25,1},{2,10},{10... | collective-permute-start | bytes 786440 | tf_op jit(solution)/shard_map/while/body/eval_jaxpr/ppermute | solution.py:25
  75.3 5.7 %collective-permute-start.3 = (bf16[256,128]{1,0:T(8,128)(2,1)S(1)}, bf16[256,128]{1,0:T(8,128)(2,1)S(1)}, u32[]{:S(2)}, u32[]{:S(2)}) collective-permute-start(bf16[256,128]{1,0:T(8,128)(2,1)S(1)} %get-tuple-element.140), channel_id=1, source_target_pairs={{1,0},{2,1},{3,2},{4,3},{5,4},{6,5},{7,6},{0,7},{9,8},{10,9},{11,1... | collective-permute-start | bytes 196616 | tf_op jit(solution)/shard_map/while/body/eval_jaxpr/ppermute | solution.py:17
  78.1 4.6 %collective-permute-start.4 = (bf16[256,128]{1,0:T(8,128)(2,1)S(1)}, bf16[256,128]{1,0:T(8,128)(2,1)S(1)}, u32[]{:S(2)}, u32[]{:S(2)}) collective-permute-start(bf16[256,128]{1,0:T(8,128)(2,1)S(1)} %get-tuple-element.141), channel_id=1, source_target_pairs={{0,1},{1,2},{2,3},{3,4},{4,5},{5,6},{6,7},{7,0},{8,9},{9,10},{10,1... | collective-permute-start | bytes 196616 | tf_op jit(solution)/shard_map/while/body/eval_jaxpr/ppermute | solution.py:16
  78.1 5.9 %collective-permute-start = (bf16[256,128]{1,0:T(8,128)(2,1)S(1)}, bf16[256,128]{1,0:T(8,128)(2,1)S(1)}, u32[]{:S(2)}, u32[]{:S(2)}) collective-permute-start(bf16[256,128]{1,0:T(8,128)(2,1)S(1)} %get-tuple-element.138), channel_id=1, source_target_pairs={{1,0},{2,1},{3,2},{4,3},{5,4},{6,5},{7,6},{0,7},{9,8},{10,9},{11,1... | collective-permute-start | bytes 196616 | tf_op jit(solution)/shard_map/while/body/eval_jaxpr/ppermute | solution.py:17
  80.8 4.6 %collective-permute-start.1 = (bf16[256,128]{1,0:T(8,128)(2,1)S(1)}, bf16[256,128]{1,0:T(8,128)(2,1)S(1)}, u32[]{:S(2)}, u32[]{:S(2)}) collective-permute-start(bf16[256,128]{1,0:T(8,128)(2,1)S(1)} %get-tuple-element.139), channel_id=1, source_target_pairs={{0,1},{1,2},{2,3},{3,4},{4,5},{5,6},{6,7},{7,0},{8,9},{9,10},{10,1... | collective-permute-start | bytes 196616 | tf_op jit(solution)/shard_map/while/body/eval_jaxpr/ppermute | solution.py:16
  83.9 9.5 %collective-permute-start.5 = (bf16[1024,128]{1,0:T(8,128)(2,1)S(1)}, bf16[1024,128]{1,0:T(8,128)(2,1)S(1)}, u32[]{:S(2)}, u32[]{:S(2)}) collective-permute-start(bf16[1024,128]{1,0:T(8,128)(2,1)S(1)} %bitcast.108), channel_id=1, source_target_pairs={{0,8},{8,16},{16,24},{24,0},{1,9},{9,17},{17,25},{25,1},{2,10},{10... | collective-permute-start | bytes 786440 | tf_op jit(solution)/shard_map/while/body/eval_jaxpr/ppermute | solution.py:25
  86.6 9.6 %collective-permute-start.2 = (bf16[1024,128]{1,0:T(8,128)(2,1)S(1)}, bf16[1024,128]{1,0:T(8,128)(2,1)S(1)}, u32[]{:S(2)}, u32[]{:S(2)}) collective-permute-start(bf16[1024,128]{1,0:T(8,128)(2,1)S(1)} %bitcast.109), channel_id=1, source_target_pairs={{0,8},{8,16},{16,24},{24,0},{1,9},{9,17},{17,25},{25,1},{2,10},{10... | collective-permute-start | bytes 786440 | tf_op jit(solution)/shard_map/while/body/eval_jaxpr/ppermute | solution.py:25
  149.8 0.9 copy-start.1
Sparse Core Ops, SparseCore 0:
  97.6 51.2 all-reduce.2
where the time goes:
time: 222 us
  waiting for transfers between devices  99.1 us (45%)
  other arithmetic  55.5 us (25%)
  starting transfers between devices  28.1 us (13%)
  local copies, waits for them, and re-layouts  16.2 us (7%)
  between operations  15.5 us (7%)
  matrix products  6.9 us (3%)
    psum x1, waiting for transfers between devices, body(): lax.psum(gram_term.astype(jnp.bfloat16), 'rows').astype(jnp.float32)  51.4 us
    ppermute x8, waiting for transfers between devices, passed_along(): return lax.ppermute(value, axis, pairs)  36.1 us
    another operation x6, other arithmetic, body(): lower_factor = jnp.linalg.cholesky(gram_total)  34 us
    ppermute x8, starting transfers between devices, with_halo(): after = lax.ppermute(leading, axis, down)  24 us
    another operation x2, other arithmetic, body(): jax.scipy.linalg.solve_triangular(lower_factor, arrived.astype(jnp.float3...  19.9 us
    ppermute x8, waiting for transfers between devices, with_halo(): before = lax.ppermute(last, axis, up)  11.6 us
    gather x8, local copies, waits for them, and re-layouts, advance(): picked = row_tiles[local_index]  5.99 us
  transfers between devices with their start and end apart: 25, of which 16 were waited for; matrix products, arithmetic and copies ran while one was open for 5% of the time, Pallas kernels for 0%

commit v1 on v0

v1 whole, which is shorter than its diff:
```python
import functools

import jax
import jax.numpy as jnp
from jax import lax
from jax.experimental import pallas as pl
from jax.experimental.pallas import tpu as pltpu
from jax.sharding import PartitionSpec as P

HB = 2
LANES = 128
MESH = pl.DeviceIdType.MESH


def when(condition):
    if condition is True:
        return lambda f: f()
    if condition is False:
        return lambda f: None
    return pl.when(condition)


def travel_kernel(
    phases, owners, reducers,
    start_ref, blocks_ref, cols_ref, counts_ref,
    arrived_ref, gram_ref,
    band, ext, prod, terms, inbox, piece, whole,
    halo_send, halo_recv, z_send, z_recv, rs_send, rs_recv, ag_send, ag_recv,
):
    block_rows, slots, tile, _ = blocks_ref.shape
    rows_here, width = start_ref.shape
    panels = width // LANES
    rim = HB * tile
    reach = 2 * HB + 1
    total_blocks = block_rows * owners
    me_z = lax.axis_index("phase")
    me = lax.axis_index("rows")
    nxt = lax.rem(me_z + 1, phases)
    prv = lax.rem(me_z + phases - 1, phases)
    right = lax.rem(me + 1, owners)
    left = lax.rem(me + owners - 1, owners)

    barrier = pltpu.get_barrier_semaphore()
    for z in (nxt, prv):
        pl.semaphore_signal(barrier, inc=1, device_id=(z, me), device_id_type=MESH)

    def greet(d, carry):
        pl.semaphore_signal(
            barrier, inc=1, device_id=(me_z, lax.rem(me + d, owners)), device_id_type=MESH
        )
        return carry

    lax.fori_loop(1, owners, greet, 0)
    for c in range(panels):
        ext[0, c, rim : rim + rows_here, :] = start_ref[:, c * LANES : (c + 1) * LANES]
    pl.semaphore_wait(barrier, owners - 1 + 2)

    own = (0, rim, rows_here)
    parts = [(0, rim), (rows_here - rim, rim)]
    if rows_here > 2 * rim:
        parts.append((rim, rows_here - 2 * rim))

    waits = []

    def send_halo(s, c, side):
        source = rim if side == 0 else rows_here
        target = rim + rows_here if side == 0 else 0
        copy = pltpu.make_async_remote_copy(
            src_ref=ext.at[s, c, pl.ds(source, rim), :],
            dst_ref=ext.at[s, c, pl.ds(target, rim), :],
            send_sem=halo_send.at[s, c, side],
            recv_sem=halo_recv.at[s, c, side],
            device_id=(me_z, left if side == 0 else right),
            device_id_type=MESH,
        )
        copy.start()
        waits.append(copy)
        return copy

    def z_copy(s, c, k):
        at, size = parts[k]
        return pltpu.make_async_remote_copy(
            src_ref=prod.at[s, c, pl.ds(at, size), :],
            dst_ref=ext.at[s + 1, c, pl.ds(rim + at, size), :],
            send_sem=z_send.at[s, c, k],
            recv_sem=z_recv.at[s, c, k],
            device_id=(nxt, me),
            device_id_type=MESH,
        )

    def multiply(s, c, i):
        prod[s, c, i * tile : (i + 1) * tile, :] = jnp.dot(
            band[i], ext[s, c, i * tile : (i + reach) * tile, :], preferred_element_type=jnp.float32
        ).astype(jnp.bfloat16)

    halos = {}
    for c in range(panels):
        for side in range(2):
            halos[0, c, side] = send_halo(0, c, side)

    nothing = jnp.zeros((tile, tile), jnp.bfloat16)
    for i in range(block_rows):
        row = me * block_rows + i
        band[i, :, HB * tile : (HB + 1) * tile] = blocks_ref[i, 0]
        for o in range(reach):
            if o == HB:
                continue
            column = lax.rem(row + (o - HB) + total_blocks, total_blocks)
            kept = nothing
            for j in range(1, slots):
                live = (cols_ref[i, j] == column) & (j < counts_ref[i])
                kept = lax.select(live, blocks_ref[i, j], kept)
            band[i, :, o * tile : (o + 1) * tile] = kept

    for s in range(phases):
        for c in range(panels):
            if s > 0:
                for k in range(2):
                    z_copy(s - 1, c, k).wait_recv()
                    halos[s, c, k] = send_halo(s, c, k)
                for k in range(2, len(parts)):
                    z_copy(s - 1, c, k).wait_recv()
            for side in range(2):
                halos[s, c, side].wait_recv()
            for k, (at, size) in enumerate(parts):
                for i in range(at // tile, (at + size) // tile):
                    multiply(s, c, i)
                copy = z_copy(s, c, k)
                copy.start()
                waits.append(copy)

    rows = (rim, rim + rows_here)
    share = width // reducers
    contract = (((0,), (0,)), ((), ()))
    for c in range(panels):
        for k in range(len(parts)):
            z_copy(phases - 1, c, k).wait_recv()
        arrived_ref[:, c * LANES : (c + 1) * LANES] = ext[phases, c, rows[0] : rows[1], :]
    arrived = arrived_ref[...]
    gram = lax.dot_general(arrived, arrived, contract, preferred_element_type=jnp.float32)
    terms[...] = gram.astype(jnp.bfloat16).reshape(reducers, share, width)

    few = owners > reducers
    i_reduce = (me < reducers) if few else True

    def rs_copy(d):
        to = lax.rem(me + d, owners)
        return pltpu.make_async_remote_copy(
            src_ref=terms.at[lax.rem(to, reducers)],
            dst_ref=inbox.at[d],
            send_sem=rs_send.at[d],
            recv_sem=rs_recv.at[d],
            device_id=(me_z, to),
            device_id_type=MESH,
        ), ((to < reducers) if few else True)

    def ag_copy(d):
        to = lax.rem(me + d, owners)
        return pltpu.make_async_remote_copy(
            src_ref=piece,
            dst_ref=whole.at[lax.rem(me, reducers)],
            send_sem=ag_send.at[d],
            recv_sem=ag_recv.at[d],
            device_id=(me_z, to),
            device_id_type=MESH,
        )

    def ag_arrival(d):
        frm = lax.rem(me + owners - d, owners)
        return pltpu.make_async_remote_copy(
            src_ref=piece,
            dst_ref=whole.at[lax.rem(frm, reducers)],
            send_sem=ag_send.at[d],
            recv_sem=ag_recv.at[d],
            device_id=(me_z, frm),
            device_id_type=MESH,
        ), ((frm < reducers) if few else True)

    for d in range(1, owners):
        copy, to_reducer = rs_copy(d)
        when(to_reducer)(copy.start)

    def reduce_piece():
        total = terms[lax.rem(me, reducers)].astype(jnp.float32)
        for d in range(1, owners):
            rs_copy(d)[0].wait_recv()
            total = total + inbox[d].astype(jnp.float32)
        total = total * (1.0 / (rows_here * owners))
        piece[...] = total
        for d in range(1, owners):
            ag_copy(d).start()
        whole[lax.rem(me, reducers)] = total

    when(i_reduce)(reduce_piece)
    for d in range(1, owners):
        copy, from_reducer = ag_arrival(d)
        when(from_reducer)(copy.wait_recv)
    gram_ref[...] = whole[...].reshape(width, width)

    for copy in waits:
        copy.wait_send()
    for d in range(1, owners):
        copy, to_reducer = rs_copy(d)
        when(to_reducer)(copy.wait_send)

    def sent():
        for d in range(1, owners):
            ag_copy(d).wait_send()

    when(i_reduce)(sent)


def travel(start, blocks, cols, counts):
    block_rows, slots, tile, _ = blocks.shape
    rows_here, width = start.shape
    phases, owners = lax.axis_size("phase"), lax.axis_size("rows")
    panels = width // LANES
    rim = HB * tile
    reducers = min(owners, width // 32)
    share = width // reducers
    part_count = 3 if rows_here > 2 * rim else 2
    dma = pltpu.SemaphoreType.DMA
    vmem = pl.BlockSpec(memory_space=pltpu.VMEM)
    smem = pl.BlockSpec(memory_space=pltpu.SMEM)
    return pl.pallas_call(
        functools.partial(travel_kernel, phases, owners, reducers),
        out_shape=(
            jax.ShapeDtypeStruct((rows_here, width), jnp.bfloat16),
            jax.ShapeDtypeStruct((width, width), jnp.float32),
        ),
        in_specs=[vmem, vmem, smem, smem],
        out_specs=(vmem, vmem),
        scratch_shapes=[
            pltpu.VMEM((block_rows, tile, (2 * HB + 1) * tile), jnp.bfloat16),
            pltpu.VMEM((phases + 1, panels, rows_here + 2 * rim, LANES), jnp.bfloat16),
            pltpu.VMEM((phases, panels, rows_here, LANES), jnp.bfloat16),
            pltpu.VMEM((reducers, share, width), jnp.bfloat16),
            pltpu.VMEM((owners, share, width), jnp.bfloat16),
            pltpu.VMEM((share, width), jnp.float32),
            pltpu.VMEM((reducers, share, width), jnp.float32),
            dma((phases, panels, 2)),
            dma((phases, panels, 2)),
            dma((phases, panels, part_count)),
            dma((phases, panels, part_count)),
            dma((owners,)),
            dma((owners,)),
            dma((owners,)),
            dma((owners,)),
        ],
        compiler_params=pltpu.CompilerParams(
            collective_id=0, has_side_effects=True, vmem_limit_bytes=48 * 1024 * 1024
        ),
        name="travel",
    )(start, blocks, cols, counts)


def ortho_kernel(panel, gram_ref, arrived_ref, basis_ref, factor_ref, upper, inverse):
    n = gram_ref.shape[0]
    leaf = 8
    row_at = lax.broadcasted_iota(jnp.int32, (n, n), 0)
    col_at = lax.broadcasted_iota(jnp.int32, (n, n), 1)
    upper[...] = gram_ref[...]
    inverse[...] = jnp.where(row_at == col_at, 1.0, 0.0).astype(jnp.float32)
    at_row = lax.broadcasted_iota(jnp.int32, (leaf, LANES), 0)

    for first in range(0, n, panel):
        lo = first // LANES * LANES
        hi = ((first + panel - 1) // LANES + 1) * LANES
        places = [(upper, t) for t in range(lo, n, LANES)] + [(inverse, t) for t in range(0, hi, LANES)]
        rest = [ref[first : first + panel, t : t + LANES] for ref, t in places]
        for base in range(first, first + panel, leaf):
            left = first + panel - base - leaf
            heads = [x[:leaf] for x in rest]
            tails = [x[leaf:] for x in rest] if left else []
            pick = base % LANES
            source = (base // LANES * LANES - lo) // LANES
            col_head = [
                jnp.broadcast_to(heads[source][:, pick + j : pick + j + 1], (leaf, LANES)) for j in range(leaf)
            ]
            col_tail = [
                jnp.broadcast_to(tails[source][:, pick + j : pick + j + 1], (left, LANES)) for j in range(leaf)
            ] if left else []
            for k in range(leaf):
                scale = lax.rsqrt(col_head[k][k : k + 1, :])
                low = col_head[k] * scale
                low_tail = col_tail[k] * scale if left else None
                for j in range(k + 1, leaf):
                    by = low[j : j + 1, :]
                    col_head[j] = col_head[j] - low * by
                    if left:
                        col_tail[j] = col_tail[j] - low_tail * by
                masked = jnp.where(at_row > k, low, 0.0)
                for t in range(len(places)):
                    row = heads[t][k : k + 1, :] * scale
                    heads[t] = jnp.where(at_row == k, row, heads[t] - masked * row)
                    if left:
                        tails[t] = tails[t] - low_tail * row
            for (ref, t), head in zip(places, heads):
                ref[base : base + leaf, t : t + LANES] = head
            rest = tails
        done = first + panel
        if done < n:
            start = done // LANES * LANES
            solved = upper[first:done, start:]
            contract = (((0,), (0,)), ((), ()))
            for ref, a, b in ((upper, start, n), (inverse, 0, hi)):
                change = lax.dot_general(
                    solved, ref[first:done, a:b], contract,
                    precision=lax.Precision.HIGHEST, preferred_element_type=jnp.float32,
                )
                ref[done:, a:b] = ref[done:, a:b] - change[done - start :]
    factor_ref[...] = jnp.where(col_at >= row_at, upper[...], 0.0)
    weights = inverse[...]
    coarse = weights.astype(jnp.bfloat16)
    fine = (weights - coarse.astype(jnp.float32)).astype(jnp.bfloat16)
    contract = (((1,), (1,)), ((), ()))
    step = n
    for at in range(0, arrived_ref.shape[0], step):
        rows = arrived_ref[at : at + step, :]
        basis_ref[at : at + step, :] = lax.dot_general(
            rows, coarse, contract, preferred_element_type=jnp.float32
        ) + lax.dot_general(rows, fine, contract, preferred_element_type=jnp.float32)


def ortho(gram, arrived, panel=32):
    n = gram.shape[0]
    vmem = pl.BlockSpec(memory_space=pltpu.VMEM)
    return pl.pallas_call(
        functools.partial(ortho_kernel, panel),
        out_shape=(
            jax.ShapeDtypeStruct(arrived.shape, jnp.float32),
            jax.ShapeDtypeStruct((n, n), jnp.float32),
        ),
        in_specs=[vmem, vmem],
        out_specs=(vmem, vmem),
        scratch_shapes=[pltpu.VMEM((n, n), jnp.float32)] * 2,
        compiler_params=pltpu.CompilerParams(vmem_limit_bytes=32 * 1024 * 1024),
        name="ortho",
    )(gram, arrived)


def body(start, blocks, cols, counts):
    arrived, gram = travel(start[0], blocks[0], cols[0], counts[0])
    basis, factor = ortho(gram, arrived)
    return (basis[None], factor[None])


def solution(mesh):
    placed = (
        P("phase", "rows", None),
        P("phase", "rows", None, None, None),
        P("phase", "rows", None),
        P("phase", "rows"),
    )
    return jax.shard_map(
        body,
        mesh=mesh,
        in_specs=placed,
        out_specs=(P("phase", "rows", None), P("phase", None, None)),
        check_vma=False,
    )
```

time: 222 us -> 81.1 us (0.37)
  waiting for transfers between devices: 99.1 us -> 0 us
  Pallas kernels: 0 us -> 76.6 us
  other arithmetic: 55.5 us -> 0 us
  starting transfers between devices: 28.1 us -> 0 us
  between operations: 15.5 us -> 0.65 us
  local copies, waits for them, and re-layouts: 16.2 us -> 3.59 us
  matrix products: 6.9 us -> 0 us
    pallas_call x0 -> x2, Pallas kernels: none -> 76.6 us  [the longest x1 66.8 us: travel(): pl.pallas_call(functools.partial(travel_kernel, phases, owners, reducers)...]
    another operation x8 -> x0, other arithmetic: 53.9 us -> none  [the longest x6 34 us: body(): lower_factor = jnp.linalg.cholesky(gram_total)]
    psum x1 -> x0, waiting for transfers between devices: 51.4 us -> none  [body(): lax.psum(gram_term.astype(jnp.bfloat16), 'rows').astype(jnp.float32)]
    ppermute x24 -> x0, waiting for transfers between devices: 47.7 us -> none  [the longest x8 36.1 us: passed_along(): return lax.ppermute(value, axis, pairs)]
    ppermute x24 -> x0, starting transfers between devices: 28.1 us -> none  [the longest x8 24 us: with_halo(): after = lax.ppermute(leading, axis, down)]
    gather x8 -> x0, local copies, waits for them, and re-layouts: 5.99 us -> none  [advance(): picked = row_tiles[local_index]]
    dot_general x9 -> x0, matrix products: 4.39 us -> none  [the longest x8 3.38 us: advance(): jnp.einsum('ijab,ijbk->iak', kept_blocks, picked, preferred_element_type=...]
    another operation x9 -> x0, local copies, waits for them, and re-layouts: 4.01 us -> none
  transfers between devices with their start and end apart: 25 -> 0, of which waited for: 16 -> 0; matrix products, arithmetic and copies ran while one was open for 5% -> 0% of each run, Pallas kernels for 0% -> 0%
where the time goes in v1:
time: 81.1 us; the launch traced here: 80.8 us
  Pallas kernels  76.6 us (94%)
  local copies, waits for them, and re-layouts  3.59 us (4%)
    pallas_call x1, Pallas kernels, travel(): pl.pallas_call(functools.partial(travel_kernel, phases, owners, reducers)...  66.8 us
    pallas_call x1, Pallas kernels, ortho(): pl.pallas_call(functools.partial(ortho_kernel, panel), out_shape=(jax.Sha...  9.74 us
    unnamed x8, local copies, waits for them, and re-layouts  3.51 us

profile of v1, /device:TPU:0, one launch (start us, length us, event | category | flops | bytes accessed | tf_op | source)
XLA Modules:
  0.0 80.8 jit_solution(6121918288113953442)
XLA Ops:
  0.6 0.0 copy-start.3
  0.6 0.7 copy-done.3
  1.3 0.0 copy-start.2
  1.3 0.1 copy.6.cols_ref
  1.4 0.6 copy-done.2
  2.0 0.0 copy-start
  2.0 1.2 %copy-done = bf16[1,8,4,128,128]{4,3,2,1,0:T(8,128)(2,1)S(1)} copy-done((bf16[1,8,4,128,128]{4,3,2,1,0:T(8,128)(2,1)S(1)}, bf16[1,8,4,128,128]{4,3,2,1,0:T(8,128)(2,1)}, u32[]{:S(2)}) %copy-start) | copy-done | bytes 1048600
  3.2 0.0 copy-start.1
  3.2 1.0 %copy-done.1 = bf16[1,1024,256]{2,1,0:T(8,128)(2,1)S(1)} copy-done((bf16[1,1024,256]{2,1,0:T(8,128)(2,1)S(1)}, bf16[1,1024,256]{2,1,0:T(8,128)(2,1)}, u32[]{:S(2)}) %copy-start.1) | copy-done | bytes 524312
  4.2 66.8 %travel.1 = (bf16[1024,256]{1,0:T(8,128)(2,1)S(1)}, f32[256,256]{1,0:T(8,128)S(1)}) custom-call(bf16[1024,256]{1,0:T(8,128)(2,1)S(1)} %bitcast.7, bf16[8,4,128,128]{3,2,1,0:T(8,128)(2,1)S(1)} %bitcast.6, s32[8,4]{1,0:T(8,128)S(1)} %copy.6.cols_ref, s32[8]{0:T(128)S(1)} %bitcast.8), custom_call_target="tpu_custom_call" | custom-call | tf_op jit(solution)/shard_map/travel/pallas_call | solution.py:225
  71.1 9.7 %ortho.1 = (f32[1024,256]{1,0:T(8,128)}, f32[256,256]{1,0:T(8,128)}) custom-call(f32[256,256]{1,0:T(8,128)S(1)} %get-tuple-element.6.gram_ref, bf16[1024,256]{1,0:T(8,128)(2,1)S(1)} %get-tuple-element.7.arrived_ref), custom_call_target="tpu_custom_call" | custom-call | tf_op jit(solution)/shard_map/ortho/pallas_call | solution.py:328
Async XLA Ops:
  0.6 0.7 copy-start.3
  1.3 0.7 copy-start.2
  2.0 1.2 %copy-start = (bf16[1,8,4,128,128]{4,3,2,1,0:T(8,128)(2,1)S(1)}, bf16[1,8,4,128,128]{4,3,2,1,0:T(8,128)(2,1)}, u32[]{:S(2)}) copy-start(bf16[1,8,4,128,128]{4,3,2,1,0:T(8,128)(2,1)} %param.5) | copy-start | bytes 3145732
  3.2 1.0 %copy-start.1 = (bf16[1,1024,256]{2,1,0:T(8,128)(2,1)S(1)}, bf16[1,1024,256]{2,1,0:T(8,128)(2,1)}, u32[]{:S(2)}) copy-start(bf16[1,1024,256]{2,1,0:T(8,128)(2,1)} %param.4) | copy-start | bytes 1572868

commit v2 on v1

--- a/solution.py
+++ b/solution.py
@@ -24,8 +24,8 @@
     phases, owners, reducers,
     start_ref, blocks_ref, cols_ref, counts_ref,
     arrived_ref, gram_ref,
-    band, ext, prod, terms, inbox, piece, whole,
-    halo_send, halo_recv, z_send, z_recv, rs_send, rs_recv, ag_send, ag_recv,
+    tiles, band, ext, prod, terms, inbox, piece, landed, whole,
+    load, halo_send, halo_recv, z_send, z_recv, rs_send, rs_recv, hop_send, hop_recv, ag_send, ag_recv,
 ):
     block_rows, slots, tile, _ = blocks_ref.shape
     rows_here, width = start_ref.shape
@@ -40,6 +40,16 @@
     right = lax.rem(me + 1, owners)
     left = lax.rem(me + owners - 1, owners)
 
+    loads = [
+        pltpu.make_async_copy(
+            start_ref.at[:, pl.ds(c * LANES, LANES)], ext.at[0, c, pl.ds(rim, rows_here), :], load.at[c]
+        )
+        for c in range(panels)
+    ]
+    loads.append(pltpu.make_async_copy(blocks_ref, tiles, load.at[panels]))
+    for copy in reversed(loads):
+        copy.start()
+
     barrier = pltpu.get_barrier_semaphore()
     for z in (nxt, prv):
         pl.semaphore_signal(barrier, inc=1, device_id=(z, me), device_id_type=MESH)
@@ -51,11 +61,26 @@
         return carry
 
     lax.fori_loop(1, owners, greet, 0)
-    for c in range(panels):
-        ext[0, c, rim : rim + rows_here, :] = start_ref[:, c * LANES : (c + 1) * LANES]
+    loads[panels].wait()
+
+    nothing = jnp.zeros((tile, tile), jnp.bfloat16)
+    for i in range(block_rows):
+        row = me * block_rows + i
+        band[i, :, HB * tile : (HB + 1) * tile] = tiles[i, 0]
+        for o in range(reach):
+            if o == HB:
+                continue
+            column = lax.rem(row + (o - HB) + total_blocks, total_blocks)
+            kept = nothing
+            for j in range(1, slots):
+                live = (cols_ref[i, j] == column) & (j < counts_ref[i])
+                kept = lax.select(live, tiles[i, j], kept)
+            band[i, :, o * tile : (o + 1) * tile] = kept
+
+    for copy in loads[:panels]:
+        copy.wait()
     pl.semaphore_wait(barrier, owners - 1 + 2)
 
-    own = (0, rim, rows_here)
     parts = [(0, rim), (rows_here - rim, rim)]
     if rows_here > 2 * rim:
         parts.append((rim, rows_here - 2 * rim))
@@ -98,20 +123,6 @@
         for side in range(2):
             halos[0, c, side] = send_halo(0, c, side)
 
-    nothing = jnp.zeros((tile, tile), jnp.bfloat16)
-    for i in range(block_rows):
-        row = me * block_rows + i
-        band[i, :, HB * tile : (HB + 1) * tile] = blocks_ref[i, 0]
-        for o in range(reach):
-            if o == HB:
-                continue
-            column = lax.rem(row + (o - HB) + total_blocks, total_blocks)
-            kept = nothing
-            for j in range(1, slots):
-                live = (cols_ref[i, j] == column) & (j < counts_ref[i])
-                kept = lax.select(live, blocks_ref[i, j], kept)
-            band[i, :, o * tile : (o + 1) * tile] = kept
-
     for s in range(phases):
         for c in range(panels):
             if s > 0:
@@ -120,24 +131,26 @@
                     halos[s, c, k] = send_halo(s, c, k)
                 for k in range(2, len(parts)):
                     z_copy(s - 1, c, k).wait_recv()
-            for side in range(2):
-                halos[s, c, side].wait_recv()
-            for k, (at, size) in enumerate(parts):
+            order = list(range(len(parts)))
+            if s == 0 and c == 0:
+                order = order[2:] + order[:2]
+            rimmed = False
+            for k in order:
+                at, size = parts[k]
+                if k < 2 and not rimmed:
+                    for side in range(2):
+                        halos[s, c, side].wait_recv()
+                    rimmed = True
                 for i in range(at // tile, (at + size) // tile):
                     multiply(s, c, i)
                 copy = z_copy(s, c, k)
                 copy.start()
                 waits.append(copy)
 
-    rows = (rim, rim + rows_here)
     share = width // reducers
     contract = (((0,), (0,)), ((), ()))
-    for c in range(panels):
-        for k in range(len(parts)):
-            z_copy(phases - 1, c, k).wait_recv()
-        arrived_ref[:, c * LANES : (c + 1) * LANES] = ext[phases, c, rows[0] : rows[1], :]
-    arrived = arrived_ref[...]
-    gram = lax.dot_general(arrived, arrived, contract, preferred_element_type=jnp.float32)
+    leaving = jnp.concatenate([prod[phases - 1, c] for c in range(panels)], axis=1)
+    gram = lax.dot_general(leaving, leaving, contract, preferred_element_type=jnp.float32)
     terms[...] = gram.astype(jnp.bfloat16).reshape(reducers, share, width)
 
     few = owners > reducers
@@ -154,10 +167,19 @@
             device_id_type=MESH,
         ), ((to < reducers) if few else True)
 
+    hop = pltpu.make_async_remote_copy(
+        src_ref=piece,
+        dst_ref=landed,
+        send_sem=hop_send.at[0],
+        recv_sem=hop_recv.at[0],
+        device_id=(nxt, me),
+        device_id_type=MESH,
+    )
+
     def ag_copy(d):
         to = lax.rem(me + d, owners)
         return pltpu.make_async_remote_copy(
-            src_ref=piece,
+            src_ref=landed,
             dst_ref=whole.at[lax.rem(me, reducers)],
             send_sem=ag_send.at[d],
             recv_sem=ag_recv.at[d],
@@ -168,7 +190,7 @@
     def ag_arrival(d):
         frm = lax.rem(me + owners - d, owners)
         return pltpu.make_async_remote_copy(
-            src_ref=piece,
+            src_ref=landed,
             dst_ref=whole.at[lax.rem(frm, reducers)],
             send_sem=ag_send.at[d],
             recv_sem=ag_recv.at[d],
@@ -185,18 +207,33 @@
         for d in range(1, owners):
             rs_copy(d)[0].wait_recv()
             total = total + inbox[d].astype(jnp.float32)
-        total = total * (1.0 / (rows_here * owners))
-        piece[...] = total
+        piece[...] = total * (1.0 / (rows_here * owners))
+        hop.start()
+
+    def spread_piece():
+        hop.wait_recv()
         for d in range(1, owners):
             ag_copy(d).start()
-        whole[lax.rem(me, reducers)] = total
+        whole[lax.rem(me, reducers)] = landed[...]
 
     when(i_reduce)(reduce_piece)
+    when(i_reduce)(spread_piece)
+    stores = []
+    for c in range(panels):
+        for k in range(len(parts)):
+            z_copy(phases - 1, c, k).wait_recv()
+        store = pltpu.make_async_copy(
+            ext.at[phases, c, pl.ds(rim, rows_here), :], arrived_ref.at[:, pl.ds(c * LANES, LANES)], load.at[c]
+        )
+        store.start()
+        stores.append(store)
     for d in range(1, owners):
         copy, from_reducer = ag_arrival(d)
         when(from_reducer)(copy.wait_recv)
     gram_ref[...] = whole[...].reshape(width, width)
 
+    for store in stores:
+        store.wait()
     for copy in waits:
         copy.wait_send()
     for d in range(1, owners):
@@ -204,6 +241,7 @@
         when(to_reducer)(copy.wait_send)
 
     def sent():
+        hop.wait_send()
         for d in range(1, owners):
             ag_copy(d).wait_send()
 
@@ -222,41 +260,51 @@
     dma = pltpu.SemaphoreType.DMA
     vmem = pl.BlockSpec(memory_space=pltpu.VMEM)
     smem = pl.BlockSpec(memory_space=pltpu.SMEM)
+    anywhere = pl.BlockSpec(memory_space=pl.ANY)
     return pl.pallas_call(
         functools.partial(travel_kernel, phases, owners, reducers),
         out_shape=(
             jax.ShapeDtypeStruct((rows_here, width), jnp.bfloat16),
             jax.ShapeDtypeStruct((width, width), jnp.float32),
         ),
-        in_specs=[vmem, vmem, smem, smem],
-        out_specs=(vmem, vmem),
+        in_specs=[anywhere, anywhere, smem, smem],
+        out_specs=(anywhere, vmem),
         scratch_shapes=[
+            pltpu.VMEM((block_rows, slots, tile, tile), jnp.bfloat16),
             pltpu.VMEM((block_rows, tile, (2 * HB + 1) * tile), jnp.bfloat16),
             pltpu.VMEM((phases + 1, panels, rows_here + 2 * rim, LANES), jnp.bfloat16),
             pltpu.VMEM((phases, panels, rows_here, LANES), jnp.bfloat16),
             pltpu.VMEM((reducers, share, width), jnp.bfloat16),
             pltpu.VMEM((owners, share, width), jnp.bfloat16),
             pltpu.VMEM((share, width), jnp.float32),
+            pltpu.VMEM((share, width), jnp.float32),
             pltpu.VMEM((reducers, share, width), jnp.float32),
+            dma((panels + 1,)),
             dma((phases, panels, 2)),
             dma((phases, panels, 2)),
             dma((phases, panels, part_count)),
             dma((phases, panels, part_count)),
             dma((owners,)),
             dma((owners,)),
+            dma((1,)),
+            dma((1,)),
             dma((owners,)),
             dma((owners,)),
         ],
         compiler_params=pltpu.CompilerParams(
-            collective_id=0, has_side_effects=True, vmem_limit_bytes=48 * 1024 * 1024
+            collective_id=0, has_side_effects=True, vmem_limit_bytes=62 * 1024 * 1024
         ),
         name="travel",
     )(start, blocks, cols, counts)
 
 
-def ortho_kernel(panel, gram_ref, arrived_ref, basis_ref, factor_ref, upper, inverse):
+def ortho_kernel(
+    panel, gram_ref, arrived_hbm, basis_hbm, factor_ref, upper, inverse, arrived_ref, basis_ref, load, store
+):
     n = gram_ref.shape[0]
     leaf = 8
+    fetch = pltpu.make_async_copy(arrived_hbm, arrived_ref, load.at[0])
+    fetch.start()
     row_at = lax.broadcasted_iota(jnp.int32, (n, n), 0)
     col_at = lax.broadcasted_iota(jnp.int32, (n, n), 1)
     upper[...] = gram_ref[...]
@@ -315,11 +363,20 @@
     fine = (weights - coarse.astype(jnp.float32)).astype(jnp.bfloat16)
     contract = (((1,), (1,)), ((), ()))
     step = n
+    fetch.wait()
+    writes = []
     for at in range(0, arrived_ref.shape[0], step):
         rows = arrived_ref[at : at + step, :]
         basis_ref[at : at + step, :] = lax.dot_general(
             rows, coarse, contract, preferred_element_type=jnp.float32
         ) + lax.dot_general(rows, fine, contract, preferred_element_type=jnp.float32)
+        write = pltpu.make_async_copy(
+            basis_ref.at[pl.ds(at, step), :], basis_hbm.at[pl.ds(at, step), :], store.at[at // step]
+        )
+        write.start()
+        writes.append(write)
+    for write in writes:
+        write.wait()
 
 
 def ortho(gram, arrived, panel=32):
@@ -331,10 +388,17 @@
             jax.ShapeDtypeStruct(arrived.shape, jnp.float32),
             jax.ShapeDtypeStruct((n, n), jnp.float32),
         ),
-        in_specs=[vmem, vmem],
-        out_specs=(vmem, vmem),
-        scratch_shapes=[pltpu.VMEM((n, n), jnp.float32)] * 2,
-        compiler_params=pltpu.CompilerParams(vmem_limit_bytes=32 * 1024 * 1024),
+        in_specs=[vmem, pl.BlockSpec(memory_space=pl.ANY)],
+        out_specs=(pl.BlockSpec(memory_space=pl.ANY), vmem),
+        scratch_shapes=[
+            pltpu.VMEM((n, n), jnp.float32),
+            pltpu.VMEM((n, n), jnp.float32),
+            pltpu.VMEM(arrived.shape, jnp.bfloat16),
+            pltpu.VMEM(arrived.shape, jnp.float32),
+            pltpu.SemaphoreType.DMA((1,)),
+            pltpu.SemaphoreType.DMA((arrived.shape[0] // n,)),
+        ],
+        compiler_params=pltpu.CompilerParams(vmem_limit_bytes=62 * 1024 * 1024),
         name="ortho",
     )(gram, arrived)
 

time: 81.1 us -> 75.5 us (0.931)
  Pallas kernels: 76.6 us -> 73.3 us
  local copies, waits for them, and re-layouts: 3.59 us -> 1.35 us
    pallas_call x1, Pallas kernels: 66.8 us -> 62 us  [travel(): pl.pallas_call(functools.partial(travel_kernel, phases, owners, reducers)...]
    unnamed x8 -> x2, local copies, waits for them, and re-layouts: 3.51 us -> 0.67 us
    pallas_call x1, Pallas kernels: 9.74 us -> 11.3 us  [ortho(): pl.pallas_call(functools.partial(ortho_kernel, panel), out_shape=(jax.Sha...]
where the time goes in v2:
time: 75.5 us; the launch traced here: 75.3 us
  Pallas kernels  73.3 us (97%)
  local copies, waits for them, and re-layouts  1.35 us (2%)
    pallas_call x1, Pallas kernels, travel(): pl.pallas_call(functools.partial(travel_kernel, phases, owners, reducers)...  62 us
    pallas_call x1, Pallas kernels, ortho(): pl.pallas_call(functools.partial(ortho_kernel, panel), out_shape=(jax.Sha...  11.3 us

profile of v2, /device:TPU:0, one launch (start us, length us, event | category | flops | bytes accessed | tf_op | source)
XLA Modules:
  0.0 75.3 jit_solution(5500141041117434550)
XLA Ops:
  0.6 0.0 copy-start
  0.6 0.7 copy-done
  1.3 0.7 copy.6.cols_ref
  2.0 62.0 %travel.1 = (bf16[1024,256]{1,0:T(8,128)(2,1)}, f32[256,256]{1,0:T(8,128)}) custom-call(bf16[1024,256]{1,0:T(8,128)(2,1)} %bitcast.7, bf16[8,4,128,128]{3,2,1,0:T(8,128)(2,1)} %bitcast.6, s32[8,4]{1,0:T(8,128)} %copy.6.cols_ref, s32[8]{0:T(128)} %bitcast.9), custom_call_target="tpu_custom_call" | custom-call | tf_op jit(solution)/shard_map/travel/pallas_call | solution.py:264
  64.0 11.3 %ortho.1 = (f32[1024,256]{1,0:T(8,128)}, f32[256,256]{1,0:T(8,128)}) custom-call(f32[256,256]{1,0:T(8,128)} %get-tuple-element.6.gram_ref, bf16[1024,256]{1,0:T(8,128)(2,1)} %get-tuple-element.7.arrived_hbm), custom_call_target="tpu_custom_call" | custom-call | tf_op jit(solution)/shard_map/ortho/pallas_call | solution.py:385
Async XLA Ops:
  0.6 0.7 copy-start

commit v3 on v2

--- a/solution.py
+++ b/solution.py
@@ -379,7 +379,7 @@
         write.wait()
 
 
-def ortho(gram, arrived, panel=32):
+def ortho(gram, arrived, panel=64):
     n = gram.shape[0]
     vmem = pl.BlockSpec(memory_space=pltpu.VMEM)
     return pl.pallas_call(

time: 75.5 us -> 75 us (level)
  no operation moved by 1% of the time
where the time goes in v3:
time: 75 us; the launch traced here: 74.7 us
  Pallas kernels  72.7 us (97%)
  local copies, waits for them, and re-layouts  1.35 us (2%)
    pallas_call x1, Pallas kernels, travel(): pl.pallas_call(functools.partial(travel_kernel, phases, owners, reducers)...  62 us
    pallas_call x1, Pallas kernels, ortho(): pl.pallas_call(functools.partial(ortho_kernel, panel), out_shape=(jax.Sha...  10.8 us

profile of v3, /device:TPU:0, one launch (start us, length us, event | category | flops | bytes accessed | tf_op | source)
XLA Modules:
  0.0 74.7 jit_solution(11544460230249153505)
XLA Ops:
  0.6 0.0 copy-start
  0.6 0.7 copy-done
  1.3 0.7 copy.6.cols_ref
  2.0 62.0 %travel.1 = (bf16[1024,256]{1,0:T(8,128)(2,1)}, f32[256,256]{1,0:T(8,128)}) custom-call(bf16[1024,256]{1,0:T(8,128)(2,1)} %bitcast.7, bf16[8,4,128,128]{3,2,1,0:T(8,128)(2,1)} %bitcast.6, s32[8,4]{1,0:T(8,128)} %copy.6.cols_ref, s32[8]{0:T(128)} %bitcast.9), custom_call_target="tpu_custom_call" | custom-call | tf_op jit(solution)/shard_map/travel/pallas_call | solution.py:264
  64.0 10.8 %ortho.1 = (f32[1024,256]{1,0:T(8,128)}, f32[256,256]{1,0:T(8,128)}) custom-call(f32[256,256]{1,0:T(8,128)} %get-tuple-element.6.gram_ref, bf16[1024,256]{1,0:T(8,128)(2,1)} %get-tuple-element.7.arrived_hbm), custom_call_target="tpu_custom_call" | custom-call | tf_op jit(solution)/shard_map/ortho/pallas_call | solution.py:385
Async XLA Ops:
  0.6 0.7 copy-start
